TPU v7x, 32 devices: a whole 2x2x4 slice. The times are simulated.
32 devices in a mesh: seq: 16 (over z, y, core), kv: 2 (over x).
Axes of the slice: x: 2, y: 2, z: 4, core: 2. Of those that a mesh axis runs over, the one named last changes fastest.
Arguments:
- plan: int32 [16], replicated, may hold values from 0 to 15, each once
- queries: bfloat16 [2048, 1024], P('seq', 'kv'), may hold values from -24 to 24
- keys: bfloat16 [2048, 256], P('seq', 'kv'), may hold values from -9 to 9
- student_c: bfloat16 [2048, 1024], P('seq', 'kv'), may hold values from -0.125 to 0.125
- layer_input: bfloat16 [2048, 8192], P('seq', 'kv'), may hold values from -6 to 6
- b_weight: bfloat16 [2, 8192, 128], P('kv'), may hold values from -0.0625 to 0.0625
Outputs:
- grad_c: bfloat16 [2048, 1024], P('seq', 'kv')
- grad_wb: float32 [2, 8192, 128], P('kv', 'seq')
Inputs may be any that keep to these rules, and one draw needn't show every extreme that they name: Each value appears once: plan[d] is the block of 128 consecutive positions held by index d of seq.
All inputs are finite; a program needn't handle non-finite values.
Results may differ from a plain program's by a relative error of at most 0.0049.
Values may be sent and summed in bfloat16 or wider, within the bound.
A program may use at most 64 MiB of HBM per device.

v0:
```python
import math
import jax
import jax.numpy as jnp
from jax import lax
from jax.sharding import PartitionSpec as P

NEG_FILL = -1e30


def block_sweep(update, running, pieces, shard_rows):
    total_rows = pieces[0].shape[0]
    shard_count = total_rows // shard_rows
    block_limit = max(1, 1024 // shard_rows)
    factor = 1
    for option in range(1, shard_count + 1):
        if shard_count % option == 0 and option <= block_limit:
            factor = option
    block_rows = factor * shard_rows
    block_count = total_rows // block_rows
    stacked = tuple(
        (member.reshape((block_count, block_rows) + member.shape[1:]) for member in pieces)
    )
    offsets = block_rows * jnp.arange(block_count, dtype=jnp.int32)

    def advance(partial_state, inputs):
        return (update(partial_state, inputs[0], inputs[1]), None)

    running, unused = lax.scan(advance, running, (stacked, offsets))
    return running


def local(plan, queries, keys, student_c, layer_input, b_weight):
    shard_rows = keys.shape[0]
    state_width = keys.shape[1]
    head_count = queries.shape[1] // state_width
    seq_count = lax.axis_size("seq")
    token_count = shard_rows * seq_count
    student_scale = 2.0 / math.sqrt(token_count)
    score_scale = 1.0 / math.sqrt(state_width)
    block_ids = jnp.arange(seq_count, dtype=jnp.int32)

    def positions_of(global_rows):
        owner_ids = global_rows // shard_rows
        picked = jnp.sum(
            jnp.where(owner_ids[:, None] == block_ids[None, :], plan[None, :], 0), axis=1
        )
        return picked * shard_rows + global_rows % shard_rows

    own_start = lax.axis_index("seq") * shard_rows
    query_pos = positions_of(own_start + jnp.arange(shard_rows, dtype=jnp.int32))
    query_heads = queries.reshape(shard_rows, head_count, state_width)
    student_heads = student_c.reshape(shard_rows, head_count, state_width)
    features = lax.all_gather(layer_input, "kv", axis=1, tiled=True)
    b_local = jnp.dot(features, b_weight[0], preferred_element_type=jnp.float32).astype(
        jnp.bfloat16
    )

    def scores_of(key_block, offset):
        key_pos = positions_of(offset + jnp.arange(key_block.shape[0], dtype=jnp.int32))
        visible = key_pos[None, None, :] <= query_pos[:, None, None]
        scores = (
            jnp.einsum("qhd,kd->qhk", query_heads, key_block, preferred_element_type=jnp.float32)
            * score_scale
        )
        return (jnp.where(visible, scores, NEG_FILL), visible)

    def stats_step(running, members, offset):
        highest, totals = running
        scores, visible = scores_of(members[0], offset)
        raised = jnp.maximum(highest, jnp.max(scores, axis=-1))
        weights = jnp.where(visible, jnp.exp(scores - raised[..., None]), 0.0)
        return (raised, totals * jnp.exp(highest - raised) + jnp.sum(weights, axis=-1))

    def pair_step(highest, totals):

        def advance_pair(running, members, offset):
            grad_acc, db_buffer = running
            key_block, b_block = members
            scores, visible = scores_of(key_block, offset)
            teacher = jnp.where(
                visible, jnp.exp(scores - highest[..., None]) / totals[..., None], 0.0
            )
            student = student_scale * jnp.einsum(
                "qhd,kd->qhk", student_heads, b_block, preferred_element_type=jnp.float32
            )
            residual = jnp.where(visible, student - teacher, 0.0).astype(jnp.bfloat16)
            grad_acc = grad_acc + jnp.einsum(
                "qhk,kd->qhd", residual, b_block, preferred_element_type=jnp.float32
            )
            contrib = jnp.einsum(
                "qhk,qhd->kd", residual, student_heads, preferred_element_type=jnp.float32
            )
            db_buffer = lax.dynamic_update_slice_in_dim(db_buffer, contrib, offset, 0)
            return (grad_acc, db_buffer)

        return advance_pair

    stats_init = (
        jnp.full((shard_rows, head_count), NEG_FILL, jnp.float32),
        jnp.zeros((shard_rows, head_count), jnp.float32),
    )
    pair_init = (
        jnp.zeros((shard_rows, head_count, state_width), jnp.float32),
        jnp.zeros((token_count, state_width), jnp.float32),
    )
    highest, totals = block_sweep(
        stats_step, stats_init, (lax.all_gather(keys, "seq", axis=0, tiled=True),), shard_rows
    )
    advance_pair = pair_step(highest, totals)
    grad_acc, db_buffer = block_sweep(
        advance_pair,
        pair_init,
        (
            lax.all_gather(keys, "seq", axis=0, tiled=True),
            lax.all_gather(b_local, "seq", axis=0, tiled=True),
        ),
        shard_rows,
    )
    arrived = lax.all_to_all(
        db_buffer.reshape(seq_count, shard_rows, state_width).astype(jnp.bfloat16),
        "seq",
        split_axis=0,
        concat_axis=0,
        tiled=True,
    ).astype(jnp.float32)
    b_grad = jnp.sum(arrived, axis=0).astype(jnp.bfloat16)
    weight_grad = lax.psum_scatter(
        jnp.einsum("td,tn->dn", features, b_grad, preferred_element_type=jnp.float32),
        "seq",
        scatter_dimension=0,
        tiled=True,
    )
    grad_c = grad_acc.reshape(shard_rows, head_count * state_width).astype(jnp.bfloat16)
    return (grad_c, weight_grad[None])


def solution(mesh):
    in_specs = (
        P(),
        P("seq", "kv"),
        P("seq", "kv"),
        P("seq", "kv"),
        P("seq", "kv"),
        P("kv", None, None),
    )
    out_specs = (P("seq", "kv"), P("kv", "seq", None))
    return jax.shard_map(local, mesh=mesh, in_specs=in_specs, out_specs=out_specs, check_vma=False)
```

profile of v0, /device:TPU:0, one launch (start us, length us, event | category | flops | bytes accessed | tf_op | source)
XLA Modules:
  0.0 205.9 jit_solution(17083190945803974519)
XLA Ops:
  9.3 26.4 %all_gather.12 = bf16[2048,128]{1,0:T(8,128)(2,1)} all-gather(bf16[128,128]{1,0:T(8,128)(2,1)} %param.12), channel_id=1, replica_groups=mesh['seq'=16,'kv'=2] {'seq'}, dimensions={0}, use_global_device_ids=true | all-gather | bytes 557056 | tf_op jit(solution)/shard_map/all_gather | solution.py:114
  37.7 15.4 %while.30 = (s32[]{:T(128)}, f32[128,4]{0,1:T(4,128)S(1)}, f32[128,4]{0,1:T(4,128)S(1)}, s32[2]{0:T(128)}, s32[16]{0:T(128)S(1)}, /*index=5*/s32[128]{0:T(128)S(...) while((s32[]{:T(128)}, f32[128,4]{0,1:T(4,128)S(1)}, ...), condition=%wide.region_5.6_spmd.clone, body=%wide.region_1.5_spmd.clone.sunk | while | flops 138624512 | bytes 5033156 | solution.py:28
  37.7 1.2 dynamic_slice.62
  40.5 2.8 %fusion.71 = (f32[128,4]{0,1:T(4,128)S(1)}, f32[1024,128,4]{1,0,2:T(8,128)}) fusion(pred[128,1024]{0,1:T(8,128)(4,1)S(1)} %broadcast_compare_fusion.4, bf16[128,4,128]{2,0,1:T(8,128)(2,1)} %get-tuple-element.599, bf16[2,1024,128]{2,1,0:T(8,128)(2,1)} %get-tuple-element.598, s32[]{:T(128)} %get-tuple-element.582), kind=kOutput, calls=%fused_computation.4.clone.1 | convolution fusion | flops 135790080 | bytes 2624000 | tf_op jit(solution)/shard_map/while/body/eval_jaxpr/qhd,kd->qhk/dot_general | solution.py:62
  43.3 2.1 %select_reduce_fusion.8 = f32[128,4]{0,1:T(4,128)S(1)} fusion(f32[1024,128,4]{1,0,2:T(8,128)} %get-tuple-element.559, f32[128,4]{0,1:T(4,128)S(1)} %select_maximum_fusion.2, pred[128,1024]{0,1:T(8,128)(4,1)S(1)} %broadcast_compare_fusion.4), kind=kLoop, calls=%fused_computation.3.clone.1 | loop fusion | flops 2620928 | bytes 2232320 | tf_op jit(solution)/shard_map/while/body/eval_jaxpr/reduce_sum | solution.py:72
  48.2 2.8 %fusion.71 = (f32[128,4]{0,1:T(4,128)S(1)}, f32[1024,128,4]{1,0,2:T(8,128)}) fusion(pred[128,1024]{0,1:T(8,128)(4,1)S(1)} %broadcast_compare_fusion.4, bf16[128,4,128]{2,0,1:T(8,128)(2,1)} %get-tuple-element.599, bf16[2,1024,128]{2,1,0:T(8,128)(2,1)} %get-tuple-element.598, s32[]{:T(128)} %get-tuple-element.582), kind=kOutput, calls=%fused_computation.4.clone.1 | convolution fusion | flops 135790080 | bytes 2624000 | tf_op jit(solution)/shard_map/while/body/eval_jaxpr/qhd,kd->qhk/dot_general | solution.py:62
  51.0 2.1 %select_reduce_fusion.8 = f32[128,4]{0,1:T(4,128)S(1)} fusion(f32[1024,128,4]{1,0,2:T(8,128)} %get-tuple-element.559, f32[128,4]{0,1:T(4,128)S(1)} %select_maximum_fusion.2, pred[128,1024]{0,1:T(8,128)(4,1)S(1)} %broadcast_compare_fusion.4), kind=kLoop, calls=%fused_computation.3.clone.1 | loop fusion | flops 2620928 | bytes 2232320 | tf_op jit(solution)/shard_map/while/body/eval_jaxpr/reduce_sum | solution.py:72
  53.2 2.3 %fusion.41 = bf16[128,128]{1,0:T(8,128)(2,1)S(1)} fusion(bf16[128,8192]{1,0:T(8,128)(2,1)} %all-gather.2.cloned.1.call-done, bf16[1,8192,128]{2,1,0:T(8,128)(2,1)S(1)} %copy-done), kind=kOutput, calls=%fused_computation.67 | convolution fusion | flops 268451840 | bytes 4227072 | tf_op jit(solution)/shard_map/dot_general | solution.py:54
  55.5 20.3 %all_gather.11 = bf16[2048,128]{1,0:T(8,128)(2,1)} all-gather(bf16[128,128]{1,0:T(8,128)(2,1)S(1)} %fusion.41), channel_id=1, replica_groups=mesh['seq'=16,'kv'=2] {'seq'}, dimensions={0}, use_global_device_ids=true | all-gather | bytes 557056 | tf_op jit(solution)/shard_map/all_gather | solution.py:115
  76.6 26.1 %while.31 = (s32[]{:T(128)}, f32[128,4,128]{2,0,1:T(8,128)}, bf16[2048,128]{1,0:T(8,128)(2,1)}, s32[2]{0:T(128)}, s32[16]{0:T(128)S(1)}, /*index=5*/s32[128]{0:T...) while((s32[]{:T(128)}, f32[128,4,128]{2,0,1:T(8,128)}, ...), condition=%wide.region_8.9_spmd.clone, body=%wide.region_6.8_spmd.clone.sunk | while | flops 541930496 | bytes 10123537 | solution.py:28
  76.6 1.3 dynamic_slice.66
  79.4 1.4 fusion.81
  80.8 2.0 fusion.83
  85.2 2.7 %dynamic_update_slice.8 = bf16[2048,128]{1,0:T(8,128)(2,1)} dynamic-update-slice(bf16[2048,128]{1,0:T(8,128)(2,1)} %get-tuple-element.619, bf16[1024,128]{1,0:T(8,128)(2,1)S(1)} %convolution_bitcast_fusion.3, s32[]{:T(128)S(6)} %select_n.206, s32[]{:T(128)} %constant.191.clone.1..sunk.1) | dynamic-update-slice | bytes 524292 | tf_op jit(solution)/shard_map/while/body/eval_jaxpr/dynamic_update_slice | solution.py:93
  87.9 2.1 %convolution_add_fusion.2 = f32[128,4,128]{2,0,1:T(8,128)} fusion(bf16[128,4,1024]{0,2,1:T(8,128)(2,1)S(1)} %fusion.83, f32[128,4,128]{2,0,1:T(8,128)} %get-tuple-element.618, bf16[2,1024,128]{2,1,0:T(8,128)(2,1)} %get-tuple-element.638, s32[]{:T(128)} %get-tuple-element.617, pred[]{:T(512)S(6)} %compare.39), kind=kOutput, calls=%fused_computation.37.clone.1 | convolution fusion | flops 134348800 | bytes 1835521 | tf_op jit(solution)/shard_map/while/body/eval_jaxpr/qhk,kd->qhd/dot_general | solution.py:87
  90.1 1.3 dynamic_slice.66
  92.9 1.4 fusion.81
  94.3 2.0 fusion.83
  98.7 1.8 dynamic_update_slice.8
  100.5 2.2 %convolution_add_fusion.2 = f32[128,4,128]{2,0,1:T(8,128)} fusion(bf16[128,4,1024]{0,2,1:T(8,128)(2,1)S(1)} %fusion.83, f32[128,4,128]{2,0,1:T(8,128)} %get-tuple-element.618, bf16[2,1024,128]{2,1,0:T(8,128)(2,1)} %get-tuple-element.638, s32[]{:T(128)} %get-tuple-element.617, pred[]{:T(512)S(6)} %compare.39), kind=kOutput, calls=%fused_computation.37.clone.1 | convolution fusion | flops 134348800 | bytes 1835521 | tf_op jit(solution)/shard_map/while/body/eval_jaxpr/qhk,kd->qhd/dot_general | solution.py:87
  102.7 18.0 %all_to_all.5 = bf16[16,128,128]{2,1,0:T(8,128)(2,1)S(1)} all-to-all(bf16[16,128,128]{2,1,0:T(8,128)(2,1)} %bitcast.107), channel_id=1, replica_groups=mesh['seq'=16,'kv'=2] {'seq'}, dimensions={0} | all-to-all | bytes 1048576 | tf_op jit(solution)/shard_map/all_to_all | solution.py:119
  120.8 4.2 %convolution_bitcast_fusion.1 = f32[8192,128]{0,1:T(8,128)} fusion(bf16[128,128]{1,0:T(8,128)(2,1)S(1)} %reduce_sum.58, bf16[128,8192]{1,0:T(8,128)(2,1)} %all-gather.2.cloned.1.call-done), kind=kOutput, calls=%fused_computation.64 | convolution fusion | flops 268435456 | bytes 6324224 | tf_op jit(solution)/shard_map/td,tn->dn/dot_general | solution.py:128
  126.6 70.7 %reduce-scatter.2.cloned.1.call-done = f32[512,128]{0,1:T(8,128)} async-done(((f32[8192,128]{0,1:T(8,128)}), f32[512,128]{0,1:T(8,128)}) %reduce-scatter.2.cloned.1.call-update) | async-done | bytes 262160 | tf_op jit(solution)/shard_map/reduce_scatter | solution.py:127
  197.3 1.8 copy.26
  (52 shorter events, 15.0 us)
Async XLA Ops:
  7.2 46.0 %copy-start = (bf16[1,8192,128]{2,1,0:T(8,128)(2,1)S(1)}, bf16[1,8192,128]{2,1,0:T(8,128)(2,1)}, u32[]{:S(2)}) copy-start(bf16[1,8192,128]{2,1,0:T(8,128)(2,1)} %param.15) | copy-start | bytes 6291460
  7.2 30.5 %copy-start.3 = (s32[16]{0:T(128)S(1)}, s32[16]{0:T(128)}, u32[]{:S(2)}) copy-start(s32[16]{0:T(128)} %param.10) | copy-start | bytes 196
  7.2 30.3 %copy-start.2 = (bf16[128,512]{1,0:T(8,128)(2,1)S(1)}, bf16[128,512]{1,0:T(8,128)(2,1)}, u32[]{:S(2)}) copy-start(bf16[128,512]{1,0:T(8,128)(2,1)} %param.13) | copy-start | bytes 393220
  7.2 45.9 %all-gather.2.cloned.1.call-start = ((), (), s32[]{:S(2)}) async-start(), calls=%async_computation.2 | async-start | bytes 3145728 | tf_op jit(solution)/shard_map/all_gather | solution.py:53
  7.9 189.4 %reduce-scatter.2.cloned.1.call-start = ((), (), s32[]{:S(2)}) async-start(), calls=%async_computation.3 | async-start | bytes 4456448 | tf_op jit(solution)/shard_map/reduce_scatter | solution.py:127
  125.0 0.9 copy-start.1
Sparse Core Ops, SparseCore 0:
  9.6 35.7 all-gather.1
  125.2 72.1 reduce-scatter.1
where the time goes:
time: 207 us; the launch traced here: 206 us
  waiting for transfers between devices  71.4 us (34%)
  blocking collectives  64.6 us (31%)
  matrix products  24.1 us (12%)
  local copies, waits for them, and re-layouts  15.1 us (7%)
  between operations  14.1 us (7%)
  other arithmetic  12.5 us (6%)
  loops' own time  4.02 us (2%)
    reduce_scatter x1, waiting for transfers between devices, local(): lax.psum_scatter(jnp.einsum('td,tn->dn', features, b_grad, preferred_elem...  70.7 us
    all_gather x1, blocking collectives, local(): lax.all_gather(keys, 'seq', axis=0, tiled=True)  26.4 us
    all_gather x1, blocking collectives, local(): lax.all_gather(b_local, 'seq', axis=0, tiled=True)  20.3 us
    all_to_all x1, blocking collectives, local(): lax.all_to_all(db_buffer.reshape(seq_count, shard_rows, state_width).asty...  18 us
    dot_general x4, matrix products, scores_of(): jnp.einsum('qhd,kd->qhk', query_heads, key_block, preferred_element_type=...  9.57 us
    dynamic_slice x4, local copies, waits for them, and re-layouts, block_sweep(): running, unused = lax.scan(advance, running, (stacked, offsets))  4.89 us
    unnamed x13, local copies, waits for them, and re-layouts  4.78 us
    dynamic_update_slice x2, local copies, waits for them, and re-layouts, advance_pair(): db_buffer = lax.dynamic_update_slice_in_dim(db_buffer, contrib, offset, 0)  4.53 us
  transfers between devices with their start and end apart: 2, of which 1 were waited for; matrix products, arithmetic and copies ran while one was open for 9% of the time, Pallas kernels for 0%

commit v1 on v0

--- a/solution.py
+++ b/solution.py
@@ -5,6 +5,27 @@
 from jax.sharding import PartitionSpec as P
 
 NEG_FILL = -1e30
+
+
+def collect(x, axis, dim):
+    count, here, rows = (lax.axis_size(axis), lax.axis_index(axis), x.shape[dim])
+    upward = [(i, (i + 1) % count) for i in range(count)]
+    left = [(i, (i - 1) % count) for i in range(count)]
+    filled = jnp.zeros((*x.shape[:dim], count * rows, *x.shape[dim + 1 :]), x.dtype)
+    filled = lax.dynamic_update_slice_in_dim(filled, x, here * rows, axis=dim)
+    from_left = from_right = x
+    middle = count // 2
+    for step in range(1, middle + 1):
+        from_left = lax.ppermute(from_left, axis, upward)
+        filled = lax.dynamic_update_slice_in_dim(
+            filled, from_left, (here - step) % count * rows, axis=dim
+        )
+        if step < count - middle:
+            from_right = lax.ppermute(from_right, axis, left)
+            filled = lax.dynamic_update_slice_in_dim(
+                filled, from_right, (here + step) % count * rows, axis=dim
+            )
+    return filled
 
 
 def block_sweep(update, running, pieces, shard_rows):
@@ -110,10 +131,7 @@
     grad_acc, db_buffer = block_sweep(
         advance_pair,
         pair_init,
-        (
-            lax.all_gather(keys, "seq", axis=0, tiled=True),
-            lax.all_gather(b_local, "seq", axis=0, tiled=True),
-        ),
+        (collect(keys, "seq", 0), lax.all_gather(b_local, "seq", axis=0, tiled=True)),
         shard_rows,
     )
     arrived = lax.all_to_all(

time: 207 us -> 251 us (1.21)
  starting transfers between devices: 0.08 us -> 32.3 us
  local copies, waits for them, and re-layouts: 15.1 us -> 26.1 us
  waiting for transfers between devices: 71.4 us -> 77.4 us
  blocking collectives: 64.6 us -> 59.1 us
    ppermute x0 -> x15, starting transfers between devices: none -> 32.3 us  [the longest x7 31.3 us: collect(): from_right = lax.ppermute(from_right, axis, left)]
    dynamic_update_slice x0 -> x16, local copies, waits for them, and re-layouts: none -> 9.78 us  [the longest x8 4.89 us: collect(): lax.dynamic_update_slice_in_dim(filled, from_left, (here - step) % count...]
    ppermute x0 -> x15, waiting for transfers between devices: none -> 7.03 us  [the longest x8 7 us: collect(): from_left = lax.ppermute(from_left, axis, upward)]
    all_gather x1, blocking collectives: 26.4 us -> 21 us  [local(): lax.all_gather(keys, 'seq', axis=0, tiled=True)]
  transfers between devices with their start and end apart: 2 -> 17, of which waited for: 1 -> 8; matrix products, arithmetic and copies ran while one was open for 9% -> 12% of each run, Pallas kernels for 0% -> 0%
where the time goes in v1:
time: 251 us; the launch traced here: 250 us
  waiting for transfers between devices  77.4 us (31%)
  blocking collectives  59.1 us (24%)
  starting transfers between devices  32.3 us (13%)
  local copies, waits for them, and re-layouts  26.1 us (10%)
  matrix products  23.9 us (10%)
  between operations  14.2 us (6%)
  other arithmetic  12.8 us (5%)
  loops' own time  4.22 us (2%)
    reduce_scatter x1, waiting for transfers between devices, local(): lax.psum_scatter(jnp.einsum('td,tn->dn', features, b_grad, preferred_elem...  70.3 us
    ppermute x7, starting transfers between devices, collect(): from_right = lax.ppermute(from_right, axis, left)  31.3 us
    all_gather x1, blocking collectives, local(): lax.all_gather(keys, 'seq', axis=0, tiled=True)  21 us
    all_gather x1, blocking collectives, local(): lax.all_gather(b_local, 'seq', axis=0, tiled=True)  20.1 us
    all_to_all x1, blocking collectives, local(): lax.all_to_all(db_buffer.reshape(seq_count, shard_rows, state_width).asty...  18 us
    dot_general x4, matrix products, scores_of(): jnp.einsum('qhd,kd->qhk', query_heads, key_block, preferred_element_type=...  9.4 us
    ppermute x8, waiting for transfers between devices, collect(): from_left = lax.ppermute(from_left, axis, upward)  7 us
    dynamic_slice x4, local copies, waits for them, and re-layouts, block_sweep(): running, unused = lax.scan(advance, running, (stacked, offsets))  5.28 us
  transfers between devices with their start and end apart: 17, of which 8 were waited for; matrix products, arithmetic and copies ran while one was open for 12% of the time, Pallas kernels for 0%

profile of v1, /device:TPU:0, one launch (start us, length us, event | category | flops | bytes accessed | tf_op | source)
XLA Modules:
  0.0 250.1 jit_solution(5469355861468666370)
XLA Ops:
  7.7 5.1 %collective-permute-start.1 = (bf16[128,128]{1,0:T(8,128)(2,1)}, bf16[128,128]{1,0:T(8,128)(2,1)S(1)}, u32[]{:S(2)}, u32[]{:S(2)}) collective-permute-start(bf16[128,128]{1,0:T(8,128)(2,1)} %param.12), channel_id=1, source_target_pairs={{0,30},{2,0},{4,2},{6,4},{8,6},{10,8},{12,10},{14,12},{16,14},{18,... | collective-permute-start | bytes 98312 | tf_op jit(solution)/shard_map/ppermute | solution.py:24
  13.5 21.0 %all_gather.11 = bf16[2048,128]{1,0:T(8,128)(2,1)S(1)} all-gather(bf16[128,128]{1,0:T(8,128)(2,1)} %param.12), channel_id=1, replica_groups=mesh['seq'=16,'kv'=2] {'seq'}, dimensions={0}, use_global_device_ids=true | all-gather | bytes 557056 | tf_op jit(solution)/shard_map/all_gather | solution.py:128
  37.0 15.5 %while.30 = (s32[]{:T(128)}, f32[128,4]{0,1:T(4,128)S(1)}, f32[128,4]{0,1:T(4,128)S(1)}, s32[2]{0:T(128)}, s32[16]{0:T(128)S(1)}, /*index=5*/s32[128]{0:T(128)S(...) while((s32[]{:T(128)}, f32[128,4]{0,1:T(4,128)S(1)}, ...), condition=%wide.region_5.6_spmd.clone, body=%wide.region_1.5_spmd.clone.sunk | while | flops 138624512 | bytes 5032648 | solution.py:49
  39.9 2.7 %fusion.71 = (f32[128,4]{0,1:T(4,128)S(1)}, f32[1024,128,4]{1,0,2:T(8,128)}) fusion(pred[128,1024]{0,1:T(8,128)(4,1)S(1)} %broadcast_compare_fusion.4, bf16[128,4,128]{2,0,1:T(8,128)(2,1)} %get-tuple-element.599, bf16[2,1024,128]{2,1,0:T(8,128)(2,1)S(1)} %get-tuple-element.598, s32[]{:T(128)} %get-tuple-element.582), kind=kOutput, calls=%fused_computation.4.clone.1 | convolution fusion | flops 135790080 | bytes 2623492 | tf_op jit(solution)/shard_map/while/body/eval_jaxpr/qhd,kd->qhk/dot_general | solution.py:83
  42.6 2.1 select_reduce_fusion.8
  47.7 2.7 %fusion.71 = (f32[128,4]{0,1:T(4,128)S(1)}, f32[1024,128,4]{1,0,2:T(8,128)}) fusion(pred[128,1024]{0,1:T(8,128)(4,1)S(1)} %broadcast_compare_fusion.4, bf16[128,4,128]{2,0,1:T(8,128)(2,1)} %get-tuple-element.599, bf16[2,1024,128]{2,1,0:T(8,128)(2,1)S(1)} %get-tuple-element.598, s32[]{:T(128)} %get-tuple-element.582), kind=kOutput, calls=%fused_computation.4.clone.1 | convolution fusion | flops 135790080 | bytes 2623492 | tf_op jit(solution)/shard_map/while/body/eval_jaxpr/qhd,kd->qhk/dot_general | solution.py:83
  50.4 2.1 select_reduce_fusion.8
  54.8 4.1 %collective-permute-start.3 = (bf16[128,128]{1,0:T(8,128)(2,1)S(1)}, bf16[128,128]{1,0:T(8,128)(2,1)S(1)}, u32[]{:S(2)}, u32[]{:S(2)}) collective-permute-start(bf16[128,128]{1,0:T(8,128)(2,1)S(1)} %collective-permute-done.1), channel_id=1, source_target_pairs={{0,30},{2,0},{4,2},{6,4},{8,6},{10,8},{12,10},{14,12},{16,14},{18,... | collective-permute-start | bytes 98312 | tf_op jit(solution)/shard_map/ppermute | solution.py:24
  60.5 4.4 %collective-permute-start.5 = (bf16[128,128]{1,0:T(8,128)(2,1)S(1)}, bf16[128,128]{1,0:T(8,128)(2,1)S(1)}, u32[]{:S(2)}, u32[]{:S(2)}) collective-permute-start(bf16[128,128]{1,0:T(8,128)(2,1)S(1)} %collective-permute-done.3), channel_id=1, source_target_pairs={{0,30},{2,0},{4,2},{6,4},{8,6},{10,8},{12,10},{14,12},{16,14},{18,... | collective-permute-start | bytes 98312 | tf_op jit(solution)/shard_map/ppermute | solution.py:24
  66.5 4.4 %collective-permute-start.7 = (bf16[128,128]{1,0:T(8,128)(2,1)S(1)}, bf16[128,128]{1,0:T(8,128)(2,1)S(1)}, u32[]{:S(2)}, u32[]{:S(2)}) collective-permute-start(bf16[128,128]{1,0:T(8,128)(2,1)S(1)} %collective-permute-done.5), channel_id=1, source_target_pairs={{0,30},{2,0},{4,2},{6,4},{8,6},{10,8},{12,10},{14,12},{16,14},{18,... | collective-permute-start | bytes 98312 | tf_op jit(solution)/shard_map/ppermute | solution.py:24
  72.5 4.4 %collective-permute-start.9 = (bf16[128,128]{1,0:T(8,128)(2,1)S(1)}, bf16[128,128]{1,0:T(8,128)(2,1)S(1)}, u32[]{:S(2)}, u32[]{:S(2)}) collective-permute-start(bf16[128,128]{1,0:T(8,128)(2,1)S(1)} %collective-permute-done.7), channel_id=1, source_target_pairs={{0,30},{2,0},{4,2},{6,4},{8,6},{10,8},{12,10},{14,12},{16,14},{18,... | collective-permute-start | bytes 98312 | tf_op jit(solution)/shard_map/ppermute | solution.py:24
  78.6 4.4 %collective-permute-start.11 = (bf16[128,128]{1,0:T(8,128)(2,1)S(1)}, bf16[128,128]{1,0:T(8,128)(2,1)S(1)}, u32[]{:S(2)}, u32[]{:S(2)}) collective-permute-start(bf16[128,128]{1,0:T(8,128)(2,1)S(1)} %collective-permute-done.9), channel_id=1, source_target_pairs={{0,30},{2,0},{4,2},{6,4},{8,6},{10,8},{12,10},{14,12},{16,14},{18,... | collective-permute-start | bytes 98312 | tf_op jit(solution)/shard_map/ppermute | solution.py:24
  84.6 4.4 %collective-permute-start.13 = (bf16[128,128]{1,0:T(8,128)(2,1)S(1)}, bf16[128,128]{1,0:T(8,128)(2,1)S(1)}, u32[]{:S(2)}, u32[]{:S(2)}) collective-permute-start(bf16[128,128]{1,0:T(8,128)(2,1)S(1)} %collective-permute-done.11), channel_id=1, source_target_pairs={{0,30},{2,0},{4,2},{6,4},{8,6},{10,8},{12,10},{14,12},{16,14},{18,... | collective-permute-start | bytes 98312 | tf_op jit(solution)/shard_map/ppermute | solution.py:24
  91.9 4.8 %collective-permute-done.14 = bf16[128,128]{1,0:T(8,128)(2,1)S(1)} collective-permute-done((bf16[128,128]{1,0:T(8,128)(2,1)S(1)}, bf16[128,128]{1,0:T(8,128)(2,1)S(1)}, u32[]{:S(2)}, u32[]{:S(2)}) %collective-permute-start.14) | collective-permute-done | bytes 32800 | tf_op jit(solution)/shard_map/ppermute | solution.py:19
  97.3 2.3 fusion.41
  99.6 20.1 %all_gather.10 = bf16[2048,128]{1,0:T(8,128)(2,1)} all-gather(bf16[128,128]{1,0:T(8,128)(2,1)S(1)} %fusion.41), channel_id=1, replica_groups=mesh['seq'=16,'kv'=2] {'seq'}, dimensions={0}, use_global_device_ids=true | all-gather | bytes 557056 | tf_op jit(solution)/shard_map/all_gather | solution.py:134
  120.6 26.6 %while.31 = (s32[]{:T(128)}, f32[128,4,128]{2,0,1:T(8,128)}, bf16[2048,128]{1,0:T(8,128)(2,1)}, s32[2]{0:T(128)}, s32[16]{0:T(128)S(1)}, /*index=5*/s32[128]{0:T...) while((s32[]{:T(128)}, f32[128,4,128]{2,0,1:T(8,128)}, ...), condition=%wide.region_8.9_spmd.clone, body=%wide.region_6.8_spmd.clone.sunk | while | flops 541930496 | bytes 10123537 | solution.py:49
  129.4 2.7 %dynamic_update_slice.88 = bf16[2048,128]{1,0:T(8,128)(2,1)} dynamic-update-slice(bf16[2048,128]{1,0:T(8,128)(2,1)} %get-tuple-element.619, bf16[1024,128]{1,0:T(8,128)(2,1)S(1)} %convolution_bitcast_fusion.3, s32[]{:T(128)S(6)} %select_n.347, s32[]{:T(128)} %constant.275.clone.1..sunk.1) | dynamic-update-slice | bytes 524292 | tf_op jit(solution)/shard_map/while/body/eval_jaxpr/dynamic_update_slice | solution.py:114
  132.1 2.1 convolution_add_fusion.2
  138.7 2.0 fusion.83
  144.9 2.2 convolution_add_fusion.2
  147.2 18.0 %all_to_all.5 = bf16[16,128,128]{2,1,0:T(8,128)(2,1)S(1)} all-to-all(bf16[16,128,128]{2,1,0:T(8,128)(2,1)} %bitcast.109), channel_id=1, replica_groups=mesh['seq'=16,'kv'=2] {'seq'}, dimensions={0} | all-to-all | bytes 1048576 | tf_op jit(solution)/shard_map/all_to_all | solution.py:137
  165.2 4.3 %convolution_bitcast_fusion.1 = f32[8192,128]{0,1:T(8,128)} fusion(bf16[128,128]{1,0:T(8,128)(2,1)S(1)} %reduce_sum.58, bf16[128,8192]{1,0:T(8,128)(2,1)} %all-gather.2.cloned.1.call-done), kind=kOutput, calls=%fused_computation.64 | convolution fusion | flops 268435456 | bytes 6324224 | tf_op jit(solution)/shard_map/td,tn->dn/dot_general | solution.py:146
  171.1 70.3 %reduce-scatter.2.cloned.1.call-done = f32[512,128]{0,1:T(8,128)} async-done(((f32[8192,128]{0,1:T(8,128)}), f32[512,128]{0,1:T(8,128)}) %reduce-scatter.2.cloned.1.call-update) | async-done | bytes 262160 | tf_op jit(solution)/shard_map/reduce_scatter | solution.py:145
  (101 shorter events, 40.8 us)
Async XLA Ops:
  7.2 90.1 %copy-start = (bf16[1,8192,128]{2,1,0:T(8,128)(2,1)S(1)}, bf16[1,8192,128]{2,1,0:T(8,128)(2,1)}, u32[]{:S(2)}) copy-start(bf16[1,8192,128]{2,1,0:T(8,128)(2,1)} %param.15) | copy-start | bytes 6291460
  7.2 29.8 %copy-start.4 = (s32[16]{0:T(128)S(1)}, s32[16]{0:T(128)}, u32[]{:S(2)}) copy-start(s32[16]{0:T(128)} %param.10) | copy-start | bytes 196
  7.2 90.1 %all-gather.2.cloned.1.call-start = ((), (), s32[]{:S(2)}) async-start(), calls=%async_computation.2 | async-start | bytes 3145728 | tf_op jit(solution)/shard_map/all_gather | solution.py:74
  7.2 47.1 %collective-permute-start = (bf16[128,128]{1,0:T(8,128)(2,1)}, bf16[128,128]{1,0:T(8,128)(2,1)S(1)}, u32[]{:S(2)}, u32[]{:S(2)}) collective-permute-start(bf16[128,128]{1,0:T(8,128)(2,1)} %param.12), channel_id=1, source_target_pairs={{0,2},{2,4},{4,6},{6,8},{8,10},{10,12},{12,14},{14,16},{16,18},{18... | collective-permute-start | bytes 98312 | tf_op jit(solution)/shard_map/ppermute | solution.py:19
  7.7 47.0 %collective-permute-start.1 = (bf16[128,128]{1,0:T(8,128)(2,1)}, bf16[128,128]{1,0:T(8,128)(2,1)S(1)}, u32[]{:S(2)}, u32[]{:S(2)}) collective-permute-start(bf16[128,128]{1,0:T(8,128)(2,1)} %param.12), channel_id=1, source_target_pairs={{0,30},{2,0},{4,2},{6,4},{8,6},{10,8},{12,10},{14,12},{16,14},{18,... | collective-permute-start | bytes 98312 | tf_op jit(solution)/shard_map/ppermute | solution.py:24
  12.8 228.6 %reduce-scatter.2.cloned.1.call-start = ((), (), s32[]{:S(2)}) async-start(), calls=%async_computation.3 | async-start | bytes 4456448 | tf_op jit(solution)/shard_map/reduce_scatter | solution.py:145
  37.0 16.4 %copy-start.2 = (bf16[128,128]{1,0:T(8,128)(2,1)S(1)}, bf16[128,128]{1,0:T(8,128)(2,1)}, u32[]{:S(2)}) copy-start(bf16[128,128]{1,0:T(8,128)(2,1)} %param.12) | copy-start | bytes 98308
  37.0 17.0 %copy-start.3 = (bf16[128,512]{1,0:T(8,128)(2,1)S(1)}, bf16[128,512]{1,0:T(8,128)(2,1)}, u32[]{:S(2)}) copy-start(bf16[128,512]{1,0:T(8,128)(2,1)} %param.13) | copy-start | bytes 393220
  54.4 6.1 %collective-permute-start.2 = (bf16[128,128]{1,0:T(8,128)(2,1)S(1)}, bf16[128,128]{1,0:T(8,128)(2,1)S(1)}, u32[]{:S(2)}, u32[]{:S(2)}) collective-permute-start(bf16[128,128]{1,0:T(8,128)(2,1)S(1)} %collective-permute-done), channel_id=1, source_target_pairs={{0,2},{2,4},{4,6},{6,8},{8,10},{10,12},{12,14},{14,16},{16,18},{18... | collective-permute-start | bytes 98312 | tf_op jit(solution)/shard_map/ppermute | solution.py:19
  54.8 5.7 %collective-permute-start.3 = (bf16[128,128]{1,0:T(8,128)(2,1)S(1)}, bf16[128,128]{1,0:T(8,128)(2,1)S(1)}, u32[]{:S(2)}, u32[]{:S(2)}) collective-permute-start(bf16[128,128]{1,0:T(8,128)(2,1)S(1)} %collective-permute-done.1), channel_id=1, source_target_pairs={{0,30},{2,0},{4,2},{6,4},{8,6},{10,8},{12,10},{14,12},{16,14},{18,... | collective-permute-start | bytes 98312 | tf_op jit(solution)/shard_map/ppermute | solution.py:24
  60.5 6.0 %collective-permute-start.4 = (bf16[128,128]{1,0:T(8,128)(2,1)S(1)}, bf16[128,128]{1,0:T(8,128)(2,1)S(1)}, u32[]{:S(2)}, u32[]{:S(2)}) collective-permute-start(bf16[128,128]{1,0:T(8,128)(2,1)S(1)} %collective-permute-done.2), channel_id=1, source_target_pairs={{0,2},{2,4},{4,6},{6,8},{8,10},{10,12},{12,14},{14,16},{16,18},{18... | collective-permute-start | bytes 98312 | tf_op jit(solution)/shard_map/ppermute | solution.py:19
  60.5 6.0 %collective-permute-start.5 = (bf16[128,128]{1,0:T(8,128)(2,1)S(1)}, bf16[128,128]{1,0:T(8,128)(2,1)S(1)}, u32[]{:S(2)}, u32[]{:S(2)}) collective-permute-start(bf16[128,128]{1,0:T(8,128)(2,1)S(1)} %collective-permute-done.3), channel_id=1, source_target_pairs={{0,30},{2,0},{4,2},{6,4},{8,6},{10,8},{12,10},{14,12},{16,14},{18,... | collective-permute-start | bytes 98312 | tf_op jit(solution)/shard_map/ppermute | solution.py:24
  66.5 6.0 %collective-permute-start.6 = (bf16[128,128]{1,0:T(8,128)(2,1)S(1)}, bf16[128,128]{1,0:T(8,128)(2,1)S(1)}, u32[]{:S(2)}, u32[]{:S(2)}) collective-permute-start(bf16[128,128]{1,0:T(8,128)(2,1)S(1)} %collective-permute-done.4), channel_id=1, source_target_pairs={{0,2},{2,4},{4,6},{6,8},{8,10},{10,12},{12,14},{14,16},{16,18},{18... | collective-permute-start | bytes 98312 | tf_op jit(solution)/shard_map/ppermute | solution.py:19
  66.5 6.0 %collective-permute-start.7 = (bf16[128,128]{1,0:T(8,128)(2,1)S(1)}, bf16[128,128]{1,0:T(8,128)(2,1)S(1)}, u32[]{:S(2)}, u32[]{:S(2)}) collective-permute-start(bf16[128,128]{1,0:T(8,128)(2,1)S(1)} %collective-permute-done.5), channel_id=1, source_target_pairs={{0,30},{2,0},{4,2},{6,4},{8,6},{10,8},{12,10},{14,12},{16,14},{18,... | collective-permute-start | bytes 98312 | tf_op jit(solution)/shard_map/ppermute | solution.py:24
  72.5 6.0 %collective-permute-start.8 = (bf16[128,128]{1,0:T(8,128)(2,1)S(1)}, bf16[128,128]{1,0:T(8,128)(2,1)S(1)}, u32[]{:S(2)}, u32[]{:S(2)}) collective-permute-start(bf16[128,128]{1,0:T(8,128)(2,1)S(1)} %collective-permute-done.6), channel_id=1, source_target_pairs={{0,2},{2,4},{4,6},{6,8},{8,10},{10,12},{12,14},{14,16},{16,18},{18... | collective-permute-start | bytes 98312 | tf_op jit(solution)/shard_map/ppermute | solution.py:19
  72.5 6.0 %collective-permute-start.9 = (bf16[128,128]{1,0:T(8,128)(2,1)S(1)}, bf16[128,128]{1,0:T(8,128)(2,1)S(1)}, u32[]{:S(2)}, u32[]{:S(2)}) collective-permute-start(bf16[128,128]{1,0:T(8,128)(2,1)S(1)} %collective-permute-done.7), channel_id=1, source_target_pairs={{0,30},{2,0},{4,2},{6,4},{8,6},{10,8},{12,10},{14,12},{16,14},{18,... | collective-permute-start | bytes 98312 | tf_op jit(solution)/shard_map/ppermute | solution.py:24
  78.6 6.0 %collective-permute-start.10 = (bf16[128,128]{1,0:T(8,128)(2,1)S(1)}, bf16[128,128]{1,0:T(8,128)(2,1)S(1)}, u32[]{:S(2)}, u32[]{:S(2)}) collective-permute-start(bf16[128,128]{1,0:T(8,128)(2,1)S(1)} %collective-permute-done.8), channel_id=1, source_target_pairs={{0,2},{2,4},{4,6},{6,8},{8,10},{10,12},{12,14},{14,16},{16,18},{18... | collective-permute-start | bytes 98312 | tf_op jit(solution)/shard_map/ppermute | solution.py:19
  78.6 6.0 %collective-permute-start.11 = (bf16[128,128]{1,0:T(8,128)(2,1)S(1)}, bf16[128,128]{1,0:T(8,128)(2,1)S(1)}, u32[]{:S(2)}, u32[]{:S(2)}) collective-permute-start(bf16[128,128]{1,0:T(8,128)(2,1)S(1)} %collective-permute-done.9), channel_id=1, source_target_pairs={{0,30},{2,0},{4,2},{6,4},{8,6},{10,8},{12,10},{14,12},{16,14},{18,... | collective-permute-start | bytes 98312 | tf_op jit(solution)/shard_map/ppermute | solution.py:24
  84.6 6.0 %collective-permute-start.12 = (bf16[128,128]{1,0:T(8,128)(2,1)S(1)}, bf16[128,128]{1,0:T(8,128)(2,1)S(1)}, u32[]{:S(2)}, u32[]{:S(2)}) collective-permute-start(bf16[128,128]{1,0:T(8,128)(2,1)S(1)} %collective-permute-done.10), channel_id=1, source_target_pairs={{0,2},{2,4},{4,6},{6,8},{8,10},{10,12},{12,14},{14,16},{16,18},{18... | collective-permute-start | bytes 98312 | tf_op jit(solution)/shard_map/ppermute | solution.py:19
  84.6 6.7 %collective-permute-start.13 = (bf16[128,128]{1,0:T(8,128)(2,1)S(1)}, bf16[128,128]{1,0:T(8,128)(2,1)S(1)}, u32[]{:S(2)}, u32[]{:S(2)}) collective-permute-start(bf16[128,128]{1,0:T(8,128)(2,1)S(1)} %collective-permute-done.11), channel_id=1, source_target_pairs={{0,30},{2,0},{4,2},{6,4},{8,6},{10,8},{12,10},{14,12},{16,14},{18,... | collective-permute-start | bytes 98312 | tf_op jit(solution)/shard_map/ppermute | solution.py:24
  90.6 6.0 %collective-permute-start.14 = (bf16[128,128]{1,0:T(8,128)(2,1)S(1)}, bf16[128,128]{1,0:T(8,128)(2,1)S(1)}, u32[]{:S(2)}, u32[]{:S(2)}) collective-permute-start(bf16[128,128]{1,0:T(8,128)(2,1)S(1)} %collective-permute-done.12), channel_id=1, source_target_pairs={{0,2},{2,4},{4,6},{6,8},{8,10},{10,12},{12,14},{14,16},{16,18},{18... | collective-permute-start | bytes 98312 | tf_op jit(solution)/shard_map/ppermute | solution.py:19
  169.5 0.9 copy-start.1
Sparse Core Ops, SparseCore 0:
  12.9 32.4 all-gather.1
  169.6 71.7 reduce-scatter.1
